TPU v7x, 32 devices: a whole 2x2x4 slice. The times are simulated.
32 devices in a mesh: dp: 16 (over z, y, core), tensor: 2 (over x).
Axes of the slice: x: 2, y: 2, z: 4, core: 2. Of those that a mesh axis runs over, the one named last changes fastest.
Arguments:
- tokens: bfloat16 [32, 1024, 768], P('dp'), may hold values from -6 to 6
- cotangent: bfloat16 [32, 1024, 768], P('dp'), may hold values from -6 to 6
- prev_att: float32 [32, 768], P('dp'), may hold values from -6 to 6
- prev_ffn: float32 [32, 768], P('dp'), may hold values from -6 to 6
- numerator_state: float32 [32, 768], P('dp', 'tensor'), may hold values from -6 to 6
- denominator_state: float32 [32, 768], P('dp', 'tensor'), may hold values from 0.5 to 4
- exponent_offset_state: float32 [32, 768], P('dp', 'tensor'), may hold values from -1 to 1
- ln1_gain: float32 [768], replicated, may hold values from 0.1 to 1.9
- ln1_bias: float32 [768], replicated, may hold values from -4 to 4
- ln2_gain: float32 [768], replicated, may hold values from 0.1 to 1.9
- ln2_bias: float32 [768], replicated, may hold values from -4 to 4
- mix_key: float32 [768], replicated, may hold values from 0.05 to 0.95
- mix_value: float32 [768], replicated, may hold values from 0.05 to 0.95
- mix_recept: float32 [768], replicated, may hold values from 0.05 to 0.95
- mix2_key: float32 [768], replicated, may hold values from 0.05 to 0.95
- mix2_recept: float32 [768], replicated, may hold values from 0.05 to 0.95
- time_decay: float32 [768], P('tensor'), may hold values from -7.5 to -1.5
- time_first: float32 [768], P('tensor'), may hold values from -1 to 1
- key_weight: bfloat16 [768, 768], P(None, 'tensor'), may hold values from -0.21875 to 0.21875
- value_weight: bfloat16 [768, 768], P(None, 'tensor'), may hold values from -0.21875 to 0.21875
- receptance_weight: bfloat16 [768, 768], P(None, 'tensor'), may hold values from -0.21875 to 0.21875
- output_weight: bfloat16 [768, 768], P('tensor'), may hold values from -0.625 to 0.625
- channel_key_weight: bfloat16 [768, 3072], P(None, 'tensor'), may hold values from -0.21875 to 0.21875
- channel_receptance_weight: bfloat16 [768, 768], P(None, 'tensor'), may hold values from -0.21875 to 0.21875
- channel_value_weight: bfloat16 [3072, 768], P('tensor'), may hold values from -0.109375 to 0.109375
Outputs:
- mixed_out: bfloat16 [32, 1024, 768], P('dp', None, 'tensor')
- grad_tokens: float32 [32, 1024, 768], P('dp')
- final_num: float32 [32, 768], P('dp', 'tensor')
- final_den: float32 [32, 768], P('dp', 'tensor')
- final_max: float32 [32, 768], P('dp', 'tensor')
- last_att: float32 [32, 768], P('dp')
- last_ffn: float32 [32, 768], P('dp')
- grad_ln1_gain: float32 [768], replicated
- grad_ln1_bias: float32 [768], replicated
- grad_ln2_gain: float32 [768], replicated
- grad_ln2_bias: float32 [768], replicated
- grad_mix_key: float32 [768], replicated
- grad_mix_value: float32 [768], replicated
- grad_mix_recept: float32 [768], replicated
- grad_mix2_key: float32 [768], replicated
- grad_mix2_recept: float32 [768], replicated
- grad_time_decay: float32 [768], replicated
- grad_time_first: float32 [768], replicated
- key_weight_gradient: float32 [768, 768], P('dp', 'tensor')
- value_weight_gradient: float32 [768, 768], P('dp', 'tensor')
- receptance_weight_gradient: float32 [768, 768], P('dp', 'tensor')
- output_weight_gradient: float32 [768, 768], P('tensor', 'dp')
- channel_key_gradient: float32 [768, 3072], P('dp', 'tensor')
- channel_receptance_gradient: float32 [768, 768], P('dp', 'tensor')
- channel_value_gradient: float32 [3072, 768], P('tensor', 'dp')
All inputs are finite; a program needn't handle non-finite values.
Results may differ from a plain program's by a relative error of at most 0.012.
Values may be sent and summed in bfloat16 or wider, within the bound.
No kernel may reach another device: no remote copies, remote signals or barrier semaphores. Data moves between devices by JAX's collectives and lax.ppermute only.
A program may use at most 192 MiB of HBM per device.

v0:
```python
import math

import jax
import jax.numpy as jnp
from jax import lax
from jax.sharding import PartitionSpec as P


def for_sending(shard):

    def short(part):
        return part.astype(jnp.bfloat16) if part.dtype == jnp.float32 else part

    return jax.tree.map(short, shard)


def layer_norm(value_matrix, gain, bias):
    center = value_matrix - jnp.mean(value_matrix, axis=-1, keepdims=True)
    spread = jnp.mean(center * center, axis=-1, keepdims=True)
    return center * lax.rsqrt(spread + 1e-05) * gain + bias


def shifted(value_matrix, previous):
    return jnp.concatenate([previous[:, None, :], value_matrix[:, :-1, :]], axis=1)


def blend(current, before, weight):
    return current * weight + before * (1.0 - weight)


def contract_product(form, left, right):
    return jnp.einsum(form, left, right, preferred_element_type=jnp.float32)


def weighted_value_blocks(
    key_matrix,
    value_matrix,
    decay_rates,
    first_token_boost,
    numerator_begin,
    denominator_begin,
    maximum_begin,
):
    segments, length, channels = key_matrix.shape
    block = math.gcd(length, 32)
    count = length // block
    rate = jnp.exp(decay_rates)
    places = jnp.arange(block, dtype=jnp.float32)
    lag_table = places[:, None] - 1.0 - places[None, :]
    earlier = places[None, :] < places[:, None]
    to_end = block - 1.0 - places

    @jax.checkpoint
    def advance(carry, pair):
        numer, denom, upper_bound = carry
        block_keys, value_block = pair
        pair_exp = block_keys[:, None, :, :] - lag_table[None, :, :, None] * rate
        pair_exp = jnp.where(earlier[None, :, :, None], pair_exp, -1e30)
        state_exp = upper_bound[:, None, :] - places[None, :, None] * rate
        self_exponential = first_token_boost + block_keys
        running_peak = jnp.maximum(
            jnp.maximum(state_exp, self_exponential), jnp.max(pair_exp, axis=2)
        )
        weights = jnp.exp(pair_exp - running_peak[:, :, None, :])
        from_state = jnp.exp(state_exp - running_peak)
        from_self = jnp.exp(self_exponential - running_peak)
        upper = (
            jnp.sum(weights * value_block[:, None, :, :], axis=2)
            + from_state * numer[:, None, :]
            + from_self * value_block
        )
        lower = jnp.sum(weights, axis=2) + from_state * denom[:, None, :] + from_self
        end_exp = block_keys - to_end[None, :, None] * rate
        carried = upper_bound - block * rate
        next_top = jnp.maximum(carried, jnp.max(end_exp, axis=1))
        keep_old = jnp.exp(carried - next_top)
        fresh = jnp.exp(end_exp - next_top[:, None, :])
        next_num = keep_old * numer + jnp.sum(fresh * value_block, axis=1)
        next_den = keep_old * denom + jnp.sum(fresh, axis=1)
        return ((next_num, next_den, next_top), upper / lower)

    def blocks_of(array):
        return jnp.swapaxes(array.reshape(segments, count, block, channels), 0, 1)

    carry, results = lax.scan(
        advance,
        (numerator_begin, denominator_begin, maximum_begin),
        (blocks_of(key_matrix), blocks_of(value_matrix)),
    )
    mixed = jnp.swapaxes(results, 0, 1).reshape(segments, length, channels)
    return (mixed, carry)


def shards(
    tokens,
    cotangent,
    prev_att,
    prev_ffn,
    numerator_state,
    denominator_state,
    exponent_offset_state,
    ln1_gain,
    ln1_bias,
    ln2_gain,
    ln2_bias,
    mix_key,
    mix_value,
    mix_recept,
    mix2_key,
    mix2_recept,
    time_decay,
    time_first,
    key_weight,
    value_weight,
    receptance_weight,
    output_weight,
    channel_key_weight,
    channel_receptance_weight,
    channel_value_weight,
):
    width = tokens.shape[2]
    half_width = key_weight.shape[1]
    col_start = lax.axis_index("tensor") * half_width
    inputs = tokens.astype(jnp.float32)

    def time_mix_in(value_matrix, gain, bias, weight_key, weight_value, weight_recept):
        normed = layer_norm(value_matrix, gain, bias)
        before = shifted(normed, prev_att)
        mixes = (
            blend(normed, before, weight_key),
            blend(normed, before, weight_value),
            blend(normed, before, weight_recept),
        )
        return (mixes, normed[:, -1])

    att_mixes, pull_att, last_att = jax.vjp(
        time_mix_in, inputs, ln1_gain, ln1_bias, mix_key, mix_value, mix_recept, has_aux=True
    )
    key_input, value_input, receptance_input = [item.astype(jnp.bfloat16) for item in att_mixes]
    key_matrix = contract_product("miy,yq->miq", key_input, key_weight)
    value_matrix = contract_product("miy,yq->miq", value_input, value_weight)
    receptance_rows = contract_product("miy,yq->miq", receptance_input, receptance_weight)

    def weighted_value_gate(
        rows_of_keys, rows_of_values, rows_of_receptance, decay_rates, first_token_boost
    ):
        mixed, finals = weighted_value_blocks(
            rows_of_keys,
            rows_of_values,
            decay_rates,
            first_token_boost,
            numerator_state,
            denominator_state,
            exponent_offset_state,
        )
        return (jax.nn.sigmoid(rows_of_receptance) * mixed, finals)

    gated, pull_wkv, finals = jax.vjp(
        weighted_value_gate,
        key_matrix,
        value_matrix,
        receptance_rows,
        time_decay,
        time_first,
        has_aux=True,
    )
    gated_reduced = gated.astype(jnp.bfloat16)
    attention_result = lax.psum(
        contract_product("znb,bk->znk", gated_reduced, output_weight), "tensor"
    )
    middle = inputs + attention_result

    def channel_mix_in(values_in, gain, bias, weight_key, weight_recept):
        normed = layer_norm(values_in, gain, bias)
        before = shifted(normed, prev_ffn)
        return (
            (blend(normed, before, weight_key), blend(normed, before, weight_recept)),
            normed[:, -1],
        )

    ffn_mixes, pull_ffn, last_ffn = jax.vjp(
        channel_mix_in, middle, ln2_gain, ln2_bias, mix2_key, mix2_recept, has_aux=True
    )
    second_key_input, second_receptance_input = [item.astype(jnp.bfloat16) for item in ffn_mixes]
    hidden_preactivation = contract_product("woa,ak->wok", second_key_input, channel_key_weight)
    hidden_activation = jnp.square(jax.nn.relu(hidden_preactivation)).astype(jnp.bfloat16)
    channel_gate = jax.nn.sigmoid(
        contract_product("miy,yq->miq", second_receptance_input, channel_receptance_weight)
    )
    weighted_value_terms = contract_product("hvc,cm->hvm", hidden_activation, channel_value_weight)
    own_values = lax.psum_scatter(
        weighted_value_terms.astype(jnp.bfloat16), "tensor", scatter_dimension=2, tiled=True
    ).astype(jnp.float32)
    own_middle = lax.dynamic_slice_in_dim(middle, col_start, half_width, 2)
    mixed_out = (own_middle + channel_gate * own_values).astype(jnp.bfloat16)
    grad_out = cotangent.astype(jnp.float32)
    own_grad = lax.dynamic_slice_in_dim(grad_out, col_start, half_width, 2)
    d_values = (own_grad * channel_gate).astype(jnp.bfloat16)
    second_receptance_gradient = (
        own_grad * own_values * channel_gate * (1.0 - channel_gate)
    ).astype(jnp.bfloat16)
    every_value_gradient = lax.all_gather(d_values, "tensor", axis=2, tiled=True)
    hidden_gradient = contract_product("vzi,mi->vzm", every_value_gradient, channel_value_weight)
    preactivation_gradient = (2.0 * jax.nn.relu(hidden_preactivation) * hidden_gradient).astype(
        jnp.bfloat16
    )
    channel_value_gradient = contract_product(
        "xov,xoa->va", hidden_activation, every_value_gradient
    )
    channel_key_gradient = contract_product("pvb,pvw->bw", second_key_input, preactivation_gradient)
    channel_receptance_gradient = contract_product(
        "qxb,qxm->bm", second_receptance_input, second_receptance_gradient
    )
    second_key_gradient = contract_product(
        "ucr,er->uce", preactivation_gradient, channel_key_weight
    )
    second_receptance_input_gradient = contract_product(
        "mgz,kz->mgk", second_receptance_gradient, channel_receptance_weight
    )
    middle_part, grad_ln2_gain, grad_ln2_bias, grad_mix2_key, grad_mix2_recept = pull_ffn(
        (second_key_gradient, second_receptance_input_gradient)
    )
    d_middle = grad_out + lax.psum(middle_part, "tensor")
    attention_gradient = d_middle.astype(jnp.bfloat16)
    output_weight_gradient = contract_product("xgn,xgq->nq", gated_reduced, attention_gradient)
    gated_gradient = contract_product("vie,ge->vig", attention_gradient, output_weight)
    keys_gradient, value_rows_gradient, receptance_gradient, grad_decay, grad_first = pull_wkv(
        gated_gradient
    )
    keys_gradient = keys_gradient.astype(jnp.bfloat16)
    value_rows_gradient = value_rows_gradient.astype(jnp.bfloat16)
    receptance_gradient = receptance_gradient.astype(jnp.bfloat16)
    key_weight_gradient = contract_product("qxb,qxm->bm", key_input, keys_gradient)
    value_weight_gradient = contract_product("qxb,qxm->bm", value_input, value_rows_gradient)
    receptance_weight_gradient = contract_product(
        "qxb,qxm->bm", receptance_input, receptance_gradient
    )
    key_input_gradient = contract_product("mgz,kz->mgk", keys_gradient, key_weight)
    value_input_gradient = contract_product("mgz,kz->mgk", value_rows_gradient, value_weight)
    receptance_input_gradient = contract_product(
        "mgz,kz->mgk", receptance_gradient, receptance_weight
    )
    input_part, grad_ln1_gain, grad_ln1_bias, grad_mix_key, grad_mix_value, grad_mix_recept = (
        pull_att((key_input_gradient, value_input_gradient, receptance_input_gradient))
    )
    grad_tokens = d_middle + jax.tree.map(
        lambda part: part.astype(jnp.float32), lax.psum(for_sending(input_part), "tensor")
    )
    empty_row = jnp.zeros((width,), jnp.float32)
    decay_full = lax.dynamic_update_slice_in_dim(empty_row, grad_decay, col_start, 0)
    first_full = lax.dynamic_update_slice_in_dim(empty_row, grad_first, col_start, 0)
    small_sums = lax.psum(
        (
            grad_ln1_gain,
            grad_ln1_bias,
            grad_ln2_gain,
            grad_ln2_bias,
            grad_mix_key,
            grad_mix_value,
            grad_mix_recept,
            grad_mix2_key,
            grad_mix2_recept,
            decay_full,
            first_full,
        ),
        ("dp", "tensor"),
    )
    big_sums = (
        lax.psum_scatter(key_weight_gradient, "dp", scatter_dimension=0, tiled=True),
        lax.psum_scatter(value_weight_gradient, "dp", scatter_dimension=0, tiled=True),
        lax.psum_scatter(receptance_weight_gradient, "dp", scatter_dimension=0, tiled=True),
        lax.psum_scatter(output_weight_gradient, "dp", scatter_dimension=1, tiled=True),
        lax.psum_scatter(channel_key_gradient, "dp", scatter_dimension=0, tiled=True),
        lax.psum_scatter(channel_receptance_gradient, "dp", scatter_dimension=0, tiled=True),
        lax.psum_scatter(channel_value_gradient, "dp", scatter_dimension=1, tiled=True),
    )
    return (
        mixed_out,
        grad_tokens,
        finals[0],
        finals[1],
        finals[2],
        last_att,
        last_ffn,
        small_sums[0],
        small_sums[1],
        small_sums[2],
        small_sums[3],
        small_sums[4],
        small_sums[5],
        small_sums[6],
        small_sums[7],
        small_sums[8],
        small_sums[9],
        small_sums[10],
        big_sums[0],
        big_sums[1],
        big_sums[2],
        big_sums[3],
        big_sums[4],
        big_sums[5],
        big_sums[6],
    )


def solution(mesh):
    return jax.shard_map(
        shards,
        mesh=mesh,
        in_specs=(
            P("dp", None, None),
            P("dp", None, None),
            P("dp", None),
            P("dp", None),
            P("dp", "tensor"),
            P("dp", "tensor"),
            P("dp", "tensor"),
            P(),
            P(),
            P(),
            P(),
            P(),
            P(),
            P(),
            P(),
            P(),
            P("tensor"),
            P("tensor"),
            P(None, "tensor"),
            P(None, "tensor"),
            P(None, "tensor"),
            P("tensor", None),
            P(None, "tensor"),
            P(None, "tensor"),
            P("tensor", None),
        ),
        out_specs=(
            P("dp", None, "tensor"),
            P("dp", None, None),
            P("dp", "tensor"),
            P("dp", "tensor"),
            P("dp", "tensor"),
            P("dp", None),
            P("dp", None),
            P(),
            P(),
            P(),
            P(),
            P(),
            P(),
            P(),
            P(),
            P(),
            P(),
            P(),
            P("dp", "tensor"),
            P("dp", "tensor"),
            P("dp", "tensor"),
            P("tensor", "dp"),
            P("dp", "tensor"),
            P("dp", "tensor"),
            P("tensor", "dp"),
        ),
        check_vma=False,
    )
```

profile of v0, /device:TPU:0, one launch (start us, length us, event | category | flops | bytes accessed | tf_op | source)
XLA Modules:
  0.0 1840.9 jit_solution(1525174542243785879)
XLA Ops:
  30.8 244.9 %while.53 = (s32[]{:T(128)}, f32[2,384]{1,0:T(2,128)S(1)}, f32[2,384]{1,0:T(2,128)S(1)}, f32[2,384]{1,0:T(2,128)S(1)}, f32[32,2,32,384]{3,2,1,0:T(8,128)}, /*ind...) while((s32[]{:T(128)}, f32[2,384]{1,0:T(2,128)S(1)}, ...), condition=%wide.region_9.10_spmd.clone.clone, body=%wide.region_2.9_spmd.clone.clone.sunk | while | flops 8040194 | bytes 7084361 | solution.py:85
  289.0 155.3 %all-reduce.7.cloned.1.call-done = f32[2,1024,768]{2,1,0:T(8,128)} async-done(((f32[2,1024,768]{2,1,0:T(8,128)}), f32[2,1024,768]{2,1,0:T(8,128)}) %all-reduce.7.cloned.1.call-update) | async-done | bytes 6291472 | tf_op jit(solution)/shard_map/psum | solution.py:168
  464.0 11.1 fusion.71
  475.1 8.9 copy.107
  493.7 38.4 %reduce-scatter.25.cloned.1.call-done = bf16[384,2048]{1,0:T(8,128)(2,1)} async-done(((bf16[768,2048]{1,0:T(8,128)(2,1)}), bf16[384,2048]{1,0:T(8,128)(2,1)}) %reduce-scatter.25.cloned.1.call-update) | async-done | bytes 1572880
  540.9 9.3 fusion.59
  550.2 9.6 all-reduce.9.cloned.1.call-start
  565.9 29.4 %all-gather.2.cloned.1.call-done = bf16[2,1024,768]{2,1,0:T(8,128)(2,1)} async-done(((bf16[2,1024,384]{2,1,0:T(8,128)(2,1)}), bf16[2,1024,768]{2,1,0:T(8,128)(2,1)}) %all-gather.2.cloned.1.call-update) | async-done | bytes 3145744 | tf_op jit(solution)/shard_map/all_gather | solution.py:202
  595.3 11.0 multiply_convert_fusion
  606.4 9.9 fusion.67
  625.1 10.5 multiply_reduce_fusion.8
  643.2 153.3 %all-reduce.9.cloned.1.call-done = f32[2,1024,768]{2,1,0:T(8,128)} async-done(((f32[2,1024,768]{2,1,0:T(8,128)}), f32[2,1024,768]{2,1,0:T(8,128)}) %all-reduce.9.cloned.1.call-update) | async-done | bytes 6291472 | tf_op jit(solution)/shard_map/psum | solution.py:223
  809.8 433.9 %while.52 = (s32[]{:T(128)}, f32[384]{0:T(512)S(1)}, f32[384]{0:T(512)S(1)}, f32[2,384]{1,0:T(2,128)S(1)}, f32[2,384]{1,0:T(2,128)S(1)}, /*index=5*/f32[2,384]{1...) while((s32[]{:T(128)}, f32[384]{0:T(512)S(1)}, ...), condition=%wide.region_39.40_spmd.clone, body=%wide.region_17.39_spmd.clone.sunk | while | flops 30872228 | bytes 20350588 | solution.py:85
  1266.1 11.8 multiply_reduce_fusion.12
  1286.6 12.5 convolution_bitcast_fusion
  1299.1 9.7 convolution_bitcast_fusion.1
  1335.1 41.5 %all-reduce.2 = (f32[768]{0:T(1024)}, f32[768]{0:T(1024)}, f32[768]{0:T(1024)}, f32[768]{0:T(1024)}, f32[768]{0:T(1024)}, /*index=5*/f32[768]{0:T(1024)}, f32[76...) all-reduce(f32[768]{0:T(1024)S(1)} %get-tuple-element.780, ...), channel_id=1, replica_groups=mesh['dp'=16,'tensor'=2] {'dp','tensor'}, use_global_device_ids=true, to_apply=%region_44.45 | all-reduce | flops 8448 | bytes 67584 | tf_op jit(solution)/shard_map/psum | solution.py:252
  1385.0 45.1 %reduce-scatter.21.cloned.1.call-done = f32[48,384]{1,0:T(8,128)} async-done(((f32[768,384]{1,0:T(8,128)}), f32[48,384]{1,0:T(8,128)}) %reduce-scatter.21.cloned.1.call-update) | async-done | bytes 73744 | tf_op jit(solution)/shard_map/reduce_scatter | solution.py:274
  1430.1 79.0 %reduce-scatter.23.cloned.1.call-done = f32[1536,48]{0,1:T(8,128)} async-done(((f32[1536,768]{0,1:T(8,128)}), f32[1536,48]{0,1:T(8,128)}) %reduce-scatter.23.cloned.1.call-update) | async-done | bytes 294928 | tf_op jit(solution)/shard_map/reduce_scatter | solution.py:275
  1509.1 79.6 %reduce-scatter.19.cloned.1.call-done = f32[48,1536]{1,0:T(8,128)} async-done(((f32[768,1536]{1,0:T(8,128)}), f32[48,1536]{1,0:T(8,128)}) %reduce-scatter.19.cloned.1.call-update) | async-done | bytes 294928 | tf_op jit(solution)/shard_map/reduce_scatter | solution.py:273
  1588.7 61.4 %reduce-scatter.15.cloned.1.call-done = f32[48,384]{1,0:T(8,128)} async-done(((f32[768,384]{1,0:T(8,128)}), f32[48,384]{1,0:T(8,128)}) %reduce-scatter.15.cloned.1.call-update) | async-done | bytes 73744 | tf_op jit(solution)/shard_map/reduce_scatter | solution.py:271
  1650.1 61.2 %reduce-scatter.17.cloned.1.call-done = f32[384,48]{0,1:T(8,128)} async-done(((f32[384,768]{0,1:T(8,128)}), f32[384,48]{0,1:T(8,128)}) %reduce-scatter.17.cloned.1.call-update) | async-done | bytes 73744 | tf_op jit(solution)/shard_map/reduce_scatter | solution.py:272
  1711.2 61.3 %reduce-scatter.11.cloned.1.call-done = f32[48,384]{1,0:T(8,128)} async-done(((f32[768,384]{1,0:T(8,128)}), f32[48,384]{1,0:T(8,128)}) %reduce-scatter.11.cloned.1.call-update) | async-done | bytes 73744 | tf_op jit(solution)/shard_map/reduce_scatter | solution.py:269
  1772.6 61.2 %reduce-scatter.13.cloned.1.call-done = f32[48,384]{1,0:T(8,128)} async-done(((f32[768,384]{1,0:T(8,128)}), f32[48,384]{1,0:T(8,128)}) %reduce-scatter.13.cloned.1.call-update) | async-done | bytes 73744 | tf_op jit(solution)/shard_map/reduce_scatter | solution.py:270
  (1888 shorter events, 848.2 us)
Async XLA Ops:
  7.2 456.8 %copy-start = (bf16[1536,768]{1,0:T(8,128)(2,1)S(1)}, bf16[1536,768]{1,0:T(8,128)(2,1)}, u32[]{:S(2)}) copy-start(bf16[1536,768]{1,0:T(8,128)(2,1)} %param.53) | copy-start | bytes 7077892
  7.3 437.0 %all-reduce.7.cloned.1.call-start = ((), (), s32[]{:S(2)}) async-start(), calls=%async_computation.8 | async-start | bytes 12582912 | tf_op jit(solution)/shard_map/psum | solution.py:168
  288.2 243.8 %reduce-scatter.25.cloned.1.call-start = ((), (), s32[]{:S(2)}) async-start(), calls=%async_computation.19 | async-start | bytes 4718592
  288.9 162.1 %copy-start.50 = (f32[2,1,768]{2,1,0:T(1,128)}, f32[2,1,768]{2,1,0:T(1,128)S(1)}, u32[]{:S(2)}) copy-start(f32[2,1,768]{2,1,0:T(1,128)S(1)} %broadcast_in_dim.214) | copy-start | bytes 18436
  289.0 162.1 %copy-start.66 = (f32[768]{0:T(1024)}, f32[768]{0:T(1024)S(1)}, u32[]{:S(2)}) copy-start(f32[768]{0:T(1024)S(1)} %get-tuple-element.929) | copy-start | bytes 9220
  289.0 162.1 %copy-start.68 = (f32[768]{0:T(1024)}, f32[768]{0:T(1024)S(1)}, u32[]{:S(2)}) copy-start(f32[768]{0:T(1024)S(1)} %get-tuple-element.930) | copy-start | bytes 9220
  488.6 106.8 %all-gather.2.cloned.1.call-start = ((), (), s32[]{:S(2)}) async-start(), calls=%async_computation.9 | async-start | bytes 4718592 | tf_op jit(solution)/shard_map/all_gather | solution.py:202
  493.7 47.2 %copy-start.26 = (bf16[768,384]{1,0:T(8,128)(2,1)S(1)}, bf16[768,384]{1,0:T(8,128)(2,1)}, u32[]{:S(2)}) copy-start(bf16[768,384]{1,0:T(8,128)(2,1)} %param.52) | copy-start | bytes 1769476
  550.2 246.2 %all-reduce.9.cloned.1.call-start = ((), (), s32[]{:S(2)}) async-start(), calls=%async_computation.10 | async-start | bytes 12582912 | tf_op jit(solution)/shard_map/psum | solution.py:223
  595.3 29.7 %slice-start = ((s8[6291456]{0:T(1024)(128)(4,1)}), s8[4194304]{0:T(1024)(128)(4,1)S(1)}, s32[]{:S(2)}) async-start(s8[6291456]{0:T(1024)(128)(4,1)} %bitcast.213), calls=%async_computation.20 | async-start | bytes 8388608
  595.3 29.7 %slice-start.2 = ((s8[6291456]{0:T(1024)(128)(4,1)}), s8[4194304]{0:T(1024)(128)(4,1)S(1)}, s32[]{:S(2)}) async-start(s8[6291456]{0:T(1024)(128)(4,1)} %bitcast.216), calls=%async_computation.22 | async-start | bytes 8388608
  606.4 18.6 %slice-start.1 = ((s8[6291456]{0:T(1024)(128)(4,1)}), s8[2097152]{0:T(1024)(128)(4,1)S(1)}, s32[]{:S(2)}) async-start(s8[6291456]{0:T(1024)(128)(4,1)} %bitcast.213), calls=%async_computation.21 | async-start | bytes 4194304
  606.4 18.6 %slice-start.3 = ((s8[6291456]{0:T(1024)(128)(4,1)}), s8[2097152]{0:T(1024)(128)(4,1)S(1)}, s32[]{:S(2)}) async-start(s8[6291456]{0:T(1024)(128)(4,1)} %bitcast.216), calls=%async_computation.23 | async-start | bytes 4194304
  643.1 733.5 %all-reduce.11.cloned.1.call-start = ((), (), s32[]{:S(2)}) async-start(), calls=%async_computation.11 | async-start | bytes 6291456 | tf_op jit(solution)/shard_map/psum | solution.py:247
  809.8 433.9 %copy-start.28 = (bf16[768,384]{1,0:T(8,128)(2,1)S(1)}, bf16[768,384]{1,0:T(8,128)(2,1)}, u32[]{:S(2)}) copy-start(bf16[768,384]{1,0:T(8,128)(2,1)} %param.47) | copy-start | bytes 1769476
  1266.1 11.8 copy-start.8
  1281.2 148.8 %reduce-scatter.21.cloned.1.call-start = ((), (), s32[]{:S(2)}) async-start(), calls=%async_computation.17 | async-start | bytes 1253376 | tf_op jit(solution)/shard_map/reduce_scatter | solution.py:274
  1286.5 222.6 %reduce-scatter.23.cloned.1.call-start = ((), (), s32[]{:S(2)}) async-start(), calls=%async_computation.18 | async-start | bytes 5013504 | tf_op jit(solution)/shard_map/reduce_scatter | solution.py:275
  1299.0 289.6 %reduce-scatter.19.cloned.1.call-start = ((), (), s32[]{:S(2)}) async-start(), calls=%async_computation.16 | async-start | bytes 5013504 | tf_op jit(solution)/shard_map/reduce_scatter | solution.py:273
  1308.8 341.2 %reduce-scatter.15.cloned.1.call-start = ((), (), s32[]{:S(2)}) async-start(), calls=%async_computation.14 | async-start | bytes 1253376 | tf_op jit(solution)/shard_map/reduce_scatter | solution.py:271
  1313.7 397.6 %reduce-scatter.17.cloned.1.call-start = ((), (), s32[]{:S(2)}) async-start(), calls=%async_computation.15 | async-start | bytes 1253376 | tf_op jit(solution)/shard_map/reduce_scatter | solution.py:272
  1321.2 451.4 %reduce-scatter.11.cloned.1.call-start = ((), (), s32[]{:S(2)}) async-start(), calls=%async_computation.12 | async-start | bytes 1253376 | tf_op jit(solution)/shard_map/reduce_scatter | solution.py:269
  1326.6 507.2 %reduce-scatter.13.cloned.1.call-start = ((), (), s32[]{:S(2)}) async-start(), calls=%async_computation.13 | async-start | bytes 1253376 | tf_op jit(solution)/shard_map/reduce_scatter | solution.py:270
  1376.6 457.2 %copy-start.1 = (bf16[1536,768]{1,0:T(8,128)(2,1)S(1)}, bf16[1536,768]{1,0:T(8,128)(2,1)}, u32[]{:S(2)}) copy-start(bf16[1536,768]{1,0:T(8,128)(2,1)} %param.53) | copy-start | bytes 7077892
  (78 other events, 391.4 us)
Sparse Core Ops, SparseCore 0:
  288.4 155.8 all-reduce.6
  488.7 43.3 reduce-scatter.24
  550.4 44.9 all-gather.1
  643.2 153.1 all-reduce.8
  1281.4 86.5 all-reduce.10
  1372.0 58.0 reduce-scatter.20
  1434.5 74.5 reduce-scatter.22
  1514.0 74.5 reduce-scatter.18
  1592.9 57.1 reduce-scatter.14
  1654.1 57.1 reduce-scatter.16
  1715.4 57.1 reduce-scatter.10
  1776.6 57.1 reduce-scatter.12
where the time goes:
time: 1860 us; the launch traced here: 1840 us
  waiting for transfers between devices  825 us (44%)
  other arithmetic  624 us (34%)
  local copies, waits for them, and re-layouts  185 us (10%)
  matrix products  133 us (7%)
  blocking collectives  41.5 us (2%)
    psum x1, waiting for transfers between devices, shards(): lax.psum(contract_product('znb,bk->znk', gated_reduced, output_weight), '...  155 us
    psum x1, waiting for transfers between devices, shards(): d_middle = grad_out + lax.psum(middle_part, 'tensor')  153 us
    dot_general x21, matrix products, contract_product(): return jnp.einsum(form, left, right, preferred_element_type=jnp.float32)  133 us
    squeeze x128, local copies, waits for them, and re-layouts, weighted_value_blocks(): lax.scan(advance, (numerator_begin, denominator_begin, maximum_begin), (b...  104 us
    reduce_sum x64, other arithmetic, advance(): jnp.sum(weights * value_block[:, None, :, :], axis=2)  102 us
    dynamic_update_slice x96, other arithmetic, weighted_value_blocks(): lax.scan(advance, (numerator_begin, denominator_begin, maximum_begin), (b...  101 us
    reduce_scatter x1, waiting for transfers between devices, shards(): lax.psum_scatter(channel_key_gradient, 'dp', scatter_dimension=0, tiled=T...  79.6 us
    reduce_scatter x1, waiting for transfers between devices, shards(): lax.psum_scatter(channel_value_gradient, 'dp', scatter_dimension=1, tiled...  79 us
  transfers between devices with their start and end apart: 12, of which 11 were waited for; matrix products, arithmetic and copies ran while one was open for 4% of the time, Pallas kernels for 0%

commit v1 on v0

v1 whole, which is shorter than its diff:
```python
import functools

import jax
import jax.numpy as jnp
from jax import lax
from jax.experimental import pallas as pl
from jax.experimental.pallas import tpu as pltpu
from jax.sharding import PartitionSpec as P

F32 = jnp.float32
BF16 = jnp.bfloat16
STEP = 8
MIB = 1 << 20


def nn(left, right):
    return jnp.dot(left, right, preferred_element_type=F32)


def nt(left, right):
    return lax.dot_general(left, right, (((1,), (1,)), ((), ())), preferred_element_type=F32)


def sigmoid(x):
    return 1.0 / (1.0 + jnp.exp(-x))


def row_sum(x):
    return jnp.sum(x, axis=0, keepdims=True)


def lane_mean(x):
    return jnp.mean(x, axis=-1, keepdims=True)


def normalize(x):
    center = x - lane_mean(x)
    scale = lax.rsqrt(lane_mean(center * center) + 1e-05)
    return center * scale, scale


def order_matrix(count, turned=False):
    chunks = count // STEP
    row = lax.broadcasted_iota(jnp.int32, (count, count), 1 if turned else 0)
    token = lax.broadcasted_iota(jnp.int32, (count, count), 0 if turned else 1)
    return (token == (row % chunks) * STEP + row // chunks).astype(BF16)


def row_before(x, first):
    chunks = x.shape[0] // STEP
    ends = x[-chunks:, :]
    rows = lax.broadcasted_iota(jnp.int32, ends.shape, 0)
    head = jnp.where(rows == 0, first, pltpu.roll(ends, 1, 0))
    return jnp.concatenate([head, x[:-chunks, :]])


def row_after(x, last):
    chunks = x.shape[0] // STEP
    starts = x[:chunks, :]
    rows = lax.broadcasted_iota(jnp.int32, starts.shape, 0)
    tail = jnp.where(rows == chunks - 1, last, pltpu.roll(starts, chunks - 1, 0))
    return jnp.concatenate([x[chunks:, :], tail])


def wkv_forward(first_block, k_ref, channel_ref, save_ref, start_ref, final_ref, carry, work):
    chunks = start_ref.shape[1]
    rate = jnp.exp(channel_ref[0:1, :])
    boost = channel_ref[1:2, :]

    @pl.when(first_block)
    def _():
        carry[0:3, :] = channel_ref[2:5, :]

    def keys(step):
        return k_ref[step * chunks : (step + 1) * chunks, :]

    peak = keys(STEP - 1)
    for step in range(STEP - 1):
        peak = jnp.maximum(peak, keys(step) - (STEP - 1.0 - step) * rate)
    number = jnp.zeros_like(peak)
    weight = jnp.zeros_like(peak)
    for step in range(STEP):
        part = jnp.exp(keys(step) - (STEP - 1.0 - step) * rate - peak)
        number = number + part * save_ref[0, step * chunks : (step + 1) * chunks, :]
        weight = weight + part
    work[0, 0:chunks, :] = peak
    top = carry[2:3, :]
    for chunk in range(chunks):
        work[1, chunk : chunk + 1, :] = top
        top = jnp.maximum(top - STEP * rate, work[0, chunk : chunk + 1, :])
    work[1, chunks : chunks + 1, :] = top
    tops = work[1, 0:chunks, :]
    later = work[1, 1 : chunks + 1, :]
    fresh = jnp.exp(peak - later)
    work[0, 0:chunks, :] = jnp.exp(tops - STEP * rate - later)
    work[2, 0:chunks, :] = fresh * number
    work[3, 0:chunks, :] = fresh * weight
    num = carry[0:1, :]
    den = carry[1:2, :]
    for chunk in range(chunks):
        at = slice(chunk, chunk + 1)
        start_ref[0, at, :] = num
        start_ref[1, at, :] = den
        num = work[0, at, :] * num + work[2, at, :]
        den = work[0, at, :] * den + work[3, at, :]
    carry[0:1, :] = num
    carry[1:2, :] = den
    carry[2:3, :] = top
    final_ref[0:3, :] = carry[0:3, :]

    num = start_ref[0, :, :]
    den = start_ref[1, :, :]
    top = tops
    for step in range(STEP):
        at = slice(step * chunks, (step + 1) * chunks)
        key = keys(step)
        value = save_ref[0, at, :]
        gap = top - (boost + key)
        small = jnp.exp(-jnp.abs(gap))
        state_wins = gap > 0
        old = jnp.where(state_wins, 1.0, small)
        now = jnp.where(state_wins, small, 1.0)
        inverse = 1.0 / (old * den + now)
        old = old * inverse
        now = now * inverse
        save_ref[1, at, :] = old * num + now * value
        save_ref[3, at, :] = old
        save_ref[4, at, :] = now
        faded = top - rate
        gap = faded - key
        small = jnp.exp(-jnp.abs(gap))
        state_wins = gap > 0
        keep = jnp.where(state_wins, 1.0, small)
        fresh = jnp.where(state_wins, small, 1.0)
        save_ref[5, at, :] = keep
        save_ref[6, at, :] = fresh
        num = keep * num + fresh * value
        den = keep * den + fresh
        top = jnp.maximum(faded, key)


def project_and_scan(inputs, weights, channel_ref, gated_ref, save_ref, start_ref, final_ref, k_ref, carry, work):
    k_ref[...] = nn(inputs[0], weights[0])
    save_ref[0, :, :] = nn(inputs[1], weights[1])
    gate = sigmoid(nn(inputs[2], weights[2]))
    save_ref[2, :, :] = gate
    wkv_forward(pl.program_id(0) == 0, k_ref, channel_ref, save_ref, start_ref, final_ref, carry, work)
    gated_ref[...] = (gate * save_ref[1, :, :]).astype(BF16)


def first_kernel(
    meta, tokens_ref, vector_ref, wk_ref, wv_ref, wr_ref, channel_ref,
    mix_ref, bound_ref, last_ref, gated_ref, save_ref, start_ref, final_ref,
    k_ref, carry, work, row,
):
    @pl.when(pl.program_id(0) == 0)
    def _():
        row[...] = vector_ref[5:6, :]

    tokens = nn(order_matrix(tokens_ref.shape[0]), tokens_ref[...])
    hat, _ = normalize(tokens)
    normed = hat * vector_ref[0:1, :] + vector_ref[1:2, :]
    first = row[...]
    bound_ref[0, :, :] = jnp.broadcast_to(first, bound_ref.shape[1:])
    before = row_before(normed, first)
    step = normed - before
    count = normed.shape[0]
    row[...] = normed[count - 1 : count, :]
    last_ref[...] = normed[count - 1 : count, :]
    mixed = [(before + step * vector_ref[2 + n : 3 + n, :]).astype(BF16) for n in range(3)]
    for n in range(3):
        mix_ref[n, :, :] = mixed[n]
    project_and_scan(
        mixed, (wk_ref[...], wv_ref[...], wr_ref[...]), channel_ref,
        gated_ref, save_ref, start_ref, final_ref, k_ref, carry, work,
    )


def second_kernel(
    mix_ref, weight_ref, channel_ref, gated_ref, save_ref, start_ref, final_ref, k_ref, carry, work
):
    project_and_scan(
        [mix_ref[n, :, :] for n in range(3)], [weight_ref[n, :, :] for n in range(3)], channel_ref,
        gated_ref, save_ref, start_ref, final_ref, k_ref, carry, work,
    )


def middle_kernel(
    meta, tokens_ref, own_ref, far_ref, wo_own_ref, wo_far_ref, vector_ref,
    middle_ref, mix_ref, bound_ref, last_ref, row,
):
    @pl.when(pl.program_id(0) == 0)
    def _():
        row[...] = vector_ref[4:5, :]

    middle = (
        nn(order_matrix(tokens_ref.shape[0]), tokens_ref[...])
        + nn(own_ref[...], wo_own_ref[...])
        + nn(far_ref[...], wo_far_ref[...])
    )
    middle_ref[...] = middle
    hat, _ = normalize(middle)
    normed = hat * vector_ref[0:1, :] + vector_ref[1:2, :]
    first = row[...]
    bound_ref[0, :, :] = jnp.broadcast_to(first, bound_ref.shape[1:])
    before = row_before(normed, first)
    step = normed - before
    count = normed.shape[0]
    row[...] = normed[count - 1 : count, :]
    last_ref[...] = normed[count - 1 : count, :]
    for n in range(2):
        mix_ref[n, :, :] = (before + step * vector_ref[2 + n : 3 + n, :]).astype(BF16)


def norm_backward(x, vectors, bound, grads, weights, row, sums_ref):
    gain, bias = vectors
    hat, scale = normalize(x)
    normed = hat * gain + bias
    step = normed - row_before(normed, bound)
    total = grads[0]
    current = grads[0] * weights[0]
    sums_ref[2:3, :] += row_sum(grads[0] * step)
    for n in range(1, len(grads)):
        total = total + grads[n]
        current = current + grads[n] * weights[n]
        sums_ref[2 + n : 3 + n, :] += row_sum(grads[n] * step)
    shifted = total - current
    flow = current + row_after(shifted, row[...])
    row[...] = shifted[0:1, :]
    sums_ref[0:1, :] += row_sum(flow * hat)
    sums_ref[1:2, :] += row_sum(flow)
    inner = flow * gain
    return scale * (inner - lane_mean(inner) - hat * lane_mean(inner * hat))


def channel_kernel(
    meta, cot_ref, middle_ref, mix_ref, bound_ref, vector_ref,
    ck_own_ref, ck_far_ref, cv_own_ref, cv_far_ref, cr_ref, wo_own_ref, wo_far_ref,
    mixed_ref, h_own_ref, h_far_ref, dp_own_ref, dp_far_ref, dval_ref, drec_ref,
    dmid_ref, datt_ref, dg_own_ref, dg_far_ref, sums_ref, row,
):
    @pl.when(pl.program_id(0) == 0)
    def _():
        row[...] = jnp.zeros_like(row)
        sums_ref[...] = jnp.zeros_like(sums_ref)

    key_in = mix_ref[0, :, :]
    relu_own = jnp.maximum(nn(key_in, ck_own_ref[...]), 0.0)
    hidden = (relu_own * relu_own).astype(BF16)
    h_own_ref[...] = hidden
    values = nn(hidden, cv_own_ref[...])
    relu_far = jnp.maximum(nn(key_in, ck_far_ref[...]), 0.0)
    hidden = (relu_far * relu_far).astype(BF16)
    h_far_ref[...] = hidden
    values = values + nn(hidden, cv_far_ref[...])
    gate = sigmoid(nn(mix_ref[1, :, :], cr_ref[...]))
    middle = middle_ref[...]
    count = middle.shape[0]
    mixed = (middle + gate * values).astype(BF16)
    mixed_ref[...] = nn(order_matrix(count, True), mixed).astype(BF16)
    grad = nn(order_matrix(count), cot_ref[...])
    passed = grad * gate
    d_values = passed.astype(BF16)
    dval_ref[...] = d_values
    d_rec = (passed * values * (1.0 - gate)).astype(BF16)
    drec_ref[...] = d_rec
    d_pre = (2.0 * relu_own * nt(d_values, cv_own_ref[...])).astype(BF16)
    dp_own_ref[...] = d_pre
    d_key = nt(d_pre, ck_own_ref[...])
    d_pre = (2.0 * relu_far * nt(d_values, cv_far_ref[...])).astype(BF16)
    dp_far_ref[...] = d_pre
    d_key = d_key + nt(d_pre, ck_far_ref[...])
    d_recept = nt(d_rec, cr_ref[...])
    d_middle = grad + norm_backward(
        middle, (vector_ref[0:1, :], vector_ref[1:2, :]), bound_ref[0, 0:1, :],
        (d_key, d_recept), (vector_ref[2:3, :], vector_ref[3:4, :]), row, sums_ref,
    )
    dmid_ref[...] = d_middle
    d_att = d_middle.astype(BF16)
    datt_ref[...] = d_att
    dg_own_ref[...] = nt(d_att, wo_own_ref[...])
    dg_far_ref[...] = nt(d_att, wo_far_ref[...])


def scan_back_kernel(
    dg_ref, save_ref, start_ref, channel_ref, out_ref, sums_ref, dy_ref, dk_ref, dv_ref, carry, work
):
    chunks = start_ref.shape[1]

    @pl.when(pl.program_id(0) == 0)
    def _():
        carry[...] = jnp.zeros_like(carry)
        sums_ref[...] = jnp.zeros_like(sums_ref)

    gate = save_ref[2, :, :]
    dy = dg_ref[...] * gate
    dy_ref[...] = dy
    out_ref[2, :, :] = (dy * save_ref[1, :, :] * (1.0 - gate)).astype(BF16)

    def at(step):
        return slice(step * chunks, (step + 1) * chunks)

    gn = jnp.zeros((chunks, dy.shape[1]), F32)
    gd = jnp.zeros_like(gn)
    product = jnp.ones_like(gn)
    for step in reversed(range(STEP)):
        part = save_ref[3, at(step), :] * dy_ref[at(step), :]
        keep = save_ref[5, at(step), :]
        gn = part + keep * gn
        gd = keep * gd - part * save_ref[1, at(step), :]
        product = product * keep
    work[0, 0:chunks, :] = gn
    work[1, 0:chunks, :] = gd
    work[2, 0:chunks, :] = product
    gn = carry[0:1, :]
    gd = carry[1:2, :]
    for chunk in reversed(range(chunks)):
        row = slice(chunk, chunk + 1)
        work[3, row, :] = gn
        work[4, row, :] = gd
        gn = work[0, row, :] + work[2, row, :] * gn
        gd = work[1, row, :] + work[2, row, :] * gd
    carry[0:1, :] = gn
    carry[1:2, :] = gd
    work[0, 0:chunks, :] = start_ref[0, :, :]
    work[1, 0:chunks, :] = start_ref[1, :, :]
    work[0, chunks : chunks + 1, :] = carry[2:3, :]
    work[1, chunks : chunks + 1, :] = carry[3:4, :]
    carry[2:3, :] = start_ref[0, 0:1, :]
    carry[3:4, :] = start_ref[1, 0:1, :]
    gn = work[3, 0:chunks, :]
    gd = work[4, 0:chunks, :]
    decay = STEP * (gn * work[0, 1 : chunks + 1, :] + gd * work[1, 1 : chunks + 1, :])
    first = jnp.zeros_like(gn)
    for step in reversed(range(STEP)):
        place = at(step)
        dy = dy_ref[place, :]
        value = save_ref[0, place, :]
        wkv = save_ref[1, place, :]
        share = save_ref[4, place, :] * dy
        bonus = share * (value - wkv)
        fresh = save_ref[6, place, :]
        through = fresh * (gn * value + gd)
        d_key = bonus + through
        dk_ref[place, :] = d_key
        dv_ref[place, :] = share + fresh * gn
        first = first + bonus
        decay = decay - through - float(step) * d_key
        part = save_ref[3, place, :] * dy
        keep = save_ref[5, place, :]
        gn = part + keep * gn
        gd = keep * gd - part * wkv
    sums_ref[0:1, :] -= row_sum(decay) * jnp.exp(channel_ref[0:1, :])
    sums_ref[1:2, :] += row_sum(first)
    out_ref[0, :, :] = dk_ref[...].astype(BF16)
    out_ref[1, :, :] = dv_ref[...].astype(BF16)


def last_kernel(
    meta, tokens_ref, dmid_ref, own_ref, far_ref, wk_ref, wv_ref, wr_ref, weight_ref, bound_ref,
    vector_ref, grad_ref, sums_ref, row,
):
    @pl.when(pl.program_id(0) == 0)
    def _():
        row[...] = jnp.zeros_like(row)
        sums_ref[...] = jnp.zeros_like(sums_ref)

    grads = [
        nt(own_ref[n, :, :], w_ref[...]) + nt(far_ref[n, :, :], weight_ref[n, :, :])
        for n, w_ref in enumerate((wk_ref, wv_ref, wr_ref))
    ]
    part = norm_backward(
        nn(order_matrix(tokens_ref.shape[0]), tokens_ref[...]), (vector_ref[0:1, :], vector_ref[1:2, :]), bound_ref[0, 0:1, :],
        grads, [vector_ref[2 + n : 3 + n, :] for n in range(3)], row, sums_ref,
    )
    grad = (dmid_ref[...] + part).astype(BF16)
    grad_ref[...] = nn(order_matrix(grad.shape[0], True), grad).astype(BF16)


def weight_gradient_kernel(order, groups, meta, left_ref, right_ref, out_ref, turned, placed):
    @pl.when(pl.program_id(1) == 0)
    def _():
        whole = left_ref.shape[1]
        for col in range(0, whole, 128):
            turned[col : col + 128, :] = left_ref[:, col : col + 128].T
        if groups > 1:
            rows = whole // groups
            for spot, other in enumerate(order):
                start = pl.multiple_of((meta[1] ^ other) * rows, rows)
                placed[spot * rows : (spot + 1) * rows, :] = turned[pl.ds(start, rows), :]

    source = placed if groups > 1 else turned
    out_ref[...] = nn(source[...], right_ref[...]).astype(BF16)


def params(mib, steps=None):
    return pltpu.CompilerParams(vmem_limit_bytes=mib * MIB, dimension_semantics=steps)


def whole(shape):
    return pl.BlockSpec(shape, lambda *_: (0,) * len(shape))


def weight_gradient(order, groups, meta, lefts, rights, tile):
    many, length, width = lefts.shape
    wide = rights.shape[2]
    tiles = wide // tile
    return pl.pallas_call(
        functools.partial(weight_gradient_kernel, order, groups),
        grid_spec=pltpu.PrefetchScalarGridSpec(
            num_scalar_prefetch=1,
            grid=(many, tiles),
            in_specs=[
                pl.BlockSpec((None, length, width), lambda m, n, meta: (m, 0, 0)),
                pl.BlockSpec((None, length, tile), lambda m, n, meta: (m, 0, n)),
            ],
            out_specs=pl.BlockSpec((width, tile), lambda m, n, meta: (0, m * tiles + n)),
            scratch_shapes=[pltpu.VMEM((width, length), BF16), pltpu.VMEM((width, length), BF16)],
        ),
        out_shape=jax.ShapeDtypeStruct((width, many * wide), BF16),
        compiler_params=params(40),
        cost_estimate=pl.CostEstimate(
            flops=2 * many * length * width * wide, bytes_accessed=4 * many * length * width, transcendentals=0
        ),
        name="weight_gradient",
    )(meta, lefts, rights)


def swapped(array):
    return lax.ppermute(array, "tensor", [(0, 1), (1, 0)])


def crossed(array, size, bit):
    return lax.ppermute(array, "dp", [(n, n ^ bit) for n in range(size)])


def added(mine, theirs, kind):
    return (mine.astype(F32) + theirs.astype(F32)).astype(kind)


def partner_copy(weight, core, size):
    rows = weight.shape[0] // 2
    half = swapped(lax.dynamic_slice_in_dim(weight, core * rows, rows, 0))
    other = crossed(half, size, 1)
    return jnp.where(core == 0, jnp.concatenate([half, other]), jnp.concatenate([other, half]))


def summed_everywhere(array, size):
    bit = 1
    array = array + crossed(array, size, bit)
    array = array + swapped(array)
    bit = 2
    while bit < size:
        array = array + crossed(array, size, bit)
        bit *= 2
    return array


def scattered_sum(own, far, size, groups):
    if groups == 1:
        total = own.astype(F32) + swapped(far).astype(F32)
        return lax.psum_scatter(total, "dp", scatter_dimension=0, tiled=True)
    half = own.shape[0] // 2
    own_in = crossed(own[half:], size, 1)
    far_in = crossed(far[half:], size, 1)
    far = added(far[:half], far_in, BF16)
    own = added(own[:half], own_in, BF16)
    own = added(own, swapped(far), BF16)
    bit = 2
    while bit < size:
        half = own.shape[0] // 2
        kind = F32 if bit * 2 == size else BF16
        own = added(own[:half], crossed(own[half:], size, bit), kind)
        bit *= 2
    return own


def shards(
    size, tokens, cotangent, prev_att, prev_ffn, numerator_state, denominator_state, exponent_offset_state,
    ln1_gain, ln1_bias, ln2_gain, ln2_bias, mix_key, mix_value, mix_recept, mix2_key, mix2_recept,
    time_decay, time_first, key_weight, value_weight, receptance_weight, output_weight,
    channel_key_weight, channel_receptance_weight, channel_value_weight,
):
    _, length, width = tokens.shape
    half = key_weight.shape[1]
    units = channel_key_weight.shape[1]
    block = min(256, length)
    blocks = length // block
    chunks = block // STEP
    side = lax.axis_index("tensor")
    place = lax.axis_index("dp")
    core = place % 2
    meta = jnp.stack([side, place]).astype(jnp.int32)
    rows = width // size
    groups = size if rows % 16 == 0 else 1
    order = []
    for spot in range(size):
        other, bit = 0, size // 2
        while bit:
            other |= (spot & 1) * bit
            spot //= 2
            bit //= 2
        order.append(other)

    def mine(array):
        return lax.dynamic_index_in_dim(array, side, 0, keepdims=False)

    def theirs(array):
        return lax.dynamic_index_in_dim(array, 1 - side, 0, keepdims=False)

    states = (numerator_state, denominator_state, exponent_offset_state)
    empty = jnp.zeros((half,), F32)
    own_channels = jnp.stack([time_decay, time_first] + [mine(item) for item in states] + [empty] * 3)
    far_channels = swapped(jnp.stack([time_decay, time_first] + [theirs(item) for item in states] + [empty] * 3))
    blank = jnp.zeros((width,), F32)
    vectors1 = jnp.stack([ln1_gain, ln1_bias, mix_key, mix_value, mix_recept, mine(prev_att), blank, blank])
    vectors2 = jnp.stack([ln2_gain, ln2_bias, mix2_key, mix2_recept, mine(prev_ffn), blank, blank, blank])

    far_kvr = jnp.stack(
        [partner_copy(item, core, size) for item in (key_weight, value_weight, receptance_weight)]
    )
    wo_far = partner_copy(output_weight, core, size)
    cr_far = partner_copy(channel_receptance_weight, core, size)
    ck_far = partner_copy(channel_key_weight, core, size)
    cv_far = partner_copy(channel_value_weight, core, size)
    cr = jnp.where(
        side == 0,
        jnp.concatenate([channel_receptance_weight, cr_far], axis=1),
        jnp.concatenate([cr_far, channel_receptance_weight], axis=1),
    )

    def segment_spec(index=lambda i: i):
        return pl.BlockSpec((None, block, width), lambda i, meta: (meta[0], index(i), 0))

    def rows_spec(columns, index=lambda i: i):
        return pl.BlockSpec((block, columns), lambda i, *_: (index(i), 0))

    def stack_spec(count, columns, index=lambda i: i, size_of=block):
        return pl.BlockSpec((count, size_of, columns), lambda i, *_: (0, index(i), 0))

    def bound_spec(index=lambda i: i):
        return pl.BlockSpec((1, 8, width), lambda i, *_: (index(i), 0, 0))

    def back(i):
        return blocks - 1 - i

    def shape(dims, kind):
        return jax.ShapeDtypeStruct(dims, kind)

    scan_shapes = [
        shape((length, half), BF16), shape((7, length, half), F32),
        shape((2, length // STEP, half), F32), shape((8, half), F32),
    ]
    scan_specs = [rows_spec(half), stack_spec(7, half), stack_spec(2, half, size_of=chunks), whole((8, half))]
    scan_scratch = [
        pltpu.VMEM((block, half), F32), pltpu.VMEM((8, half), F32), pltpu.VMEM((4, chunks + 8, half), F32),
    ]
    mix1, bounds1, last_att, gated_own, save_own, start_own, final_own = pl.pallas_call(
        first_kernel,
        grid_spec=pltpu.PrefetchScalarGridSpec(
            num_scalar_prefetch=1,
            grid=(blocks,),
            in_specs=[segment_spec(), whole((8, width))] + [whole((width, half))] * 3 + [whole((8, half))],
            out_specs=[stack_spec(3, width), bound_spec(), whole((1, width))] + scan_specs,
            scratch_shapes=scan_scratch + [pltpu.VMEM((1, width), F32)],
        ),
        out_shape=[
            shape((3, length, width), BF16), shape((blocks, 8, width), F32), shape((1, width), F32),
        ] + scan_shapes,
        compiler_params=params(48),
        name="time_mix_own",
    )(meta, tokens, vectors1, key_weight, value_weight, receptance_weight, own_channels)

    gated_far, save_far, start_far, final_far = pl.pallas_call(
        second_kernel,
        grid=(blocks,),
        in_specs=[stack_spec(3, width), whole((3, width, half)), whole((8, half))],
        out_specs=scan_specs,
        out_shape=scan_shapes,
        scratch_shapes=scan_scratch,
        compiler_params=params(48),
        name="time_mix_far",
    )(mix1, far_kvr, far_channels)

    middle, mix2, bounds2, last_ffn = pl.pallas_call(
        middle_kernel,
        grid_spec=pltpu.PrefetchScalarGridSpec(
            num_scalar_prefetch=1,
            grid=(blocks,),
            in_specs=[segment_spec(), rows_spec(half), rows_spec(half)]
            + [whole((half, width))] * 2 + [whole((8, width))],
            out_specs=[rows_spec(width), stack_spec(2, width), bound_spec(), whole((1, width))],
            scratch_shapes=[pltpu.VMEM((1, width), F32)],
        ),
        out_shape=[
            shape((length, width), F32), shape((2, length, width), BF16),
            shape((blocks, 8, width), F32), shape((1, width), F32),
        ],
        compiler_params=params(48),
        name="middle",
    )(meta, tokens, gated_own, gated_far, output_weight, wo_far, vectors2)

    (
        mixed, h_own, h_far, dpre_own, dpre_far, d_values, d_rec, d_middle, d_att, dg_own, dg_far, sums2,
    ) = pl.pallas_call(
        channel_kernel,
        grid_spec=pltpu.PrefetchScalarGridSpec(
            num_scalar_prefetch=1,
            grid=(blocks,),
            in_specs=[
                segment_spec(back), rows_spec(width, back), stack_spec(2, width, back), bound_spec(back),
                whole((8, width)), whole((width, units)), whole((width, units)),
                whole((units, width)), whole((units, width)), whole((width, width)),
                whole((half, width)), whole((half, width)),
            ],
            out_specs=[
                rows_spec(width, back), rows_spec(units, back), rows_spec(units, back),
                rows_spec(units, back), rows_spec(units, back), rows_spec(width, back),
                rows_spec(width, back), rows_spec(width, back), rows_spec(width, back),
                rows_spec(half, back), rows_spec(half, back), whole((8, width)),
            ],
            scratch_shapes=[pltpu.VMEM((1, width), F32)],
        ),
        out_shape=[
            shape((length, width), BF16), shape((length, units), BF16), shape((length, units), BF16),
            shape((length, units), BF16), shape((length, units), BF16), shape((length, width), BF16),
            shape((length, width), BF16), shape((length, width), F32), shape((length, width), BF16),
            shape((length, half), F32), shape((length, half), F32), shape((8, width), F32),
        ],
        compiler_params=params(60),
        name="channel_mix",
    )(
        meta, cotangent, middle, mix2, bounds2, vectors2, channel_key_weight, ck_far,
        channel_value_weight, cv_far, cr, output_weight, wo_far,
    )

    def gradients(left, right, tile):
        return weight_gradient(order, groups, meta, left, right, tile)

    def halves(array, axis):
        own = lax.dynamic_slice_in_dim(array, side * half, half, axis)
        far = lax.dynamic_slice_in_dim(array, (1 - side) * half, half, axis)
        return own, far

    g_ck = [gradients(mix2[0:1], item[None], 512) for item in (dpre_own, dpre_far)]
    g_cv = [gradients(d_values[None], item[None], 512) for item in (h_own, h_far)]
    g_cr = [gradients(mix2[1:2], item[None], half) for item in halves(d_rec, 1)]
    g_wo = [gradients(d_att[None], item[None], half) for item in (gated_own, gated_far)]

    def scan_back(grads, saved, starts, channels):
        return pl.pallas_call(
            scan_back_kernel,
            grid=(blocks,),
            in_specs=[
                rows_spec(half, back), stack_spec(7, half, back),
                stack_spec(2, half, back, size_of=chunks), whole((8, half)),
            ],
            out_specs=[stack_spec(3, half, back), whole((8, half))],
            out_shape=[shape((3, length, half), BF16), shape((8, half), F32)],
            scratch_shapes=[pltpu.VMEM((block, half), F32)] * 3
            + [pltpu.VMEM((8, half), F32), pltpu.VMEM((5, chunks + 8, half), F32)],
            compiler_params=params(48),
            name="scan_back",
        )(grads, saved, starts, channels)

    d_far, channel_sums_far = scan_back(dg_far, save_far, start_far, far_channels)
    d_own, channel_sums_own = scan_back(dg_own, save_own, start_own, own_channels)
    g_kvr = [gradients(mix1, item, half) for item in (d_own, d_far)]

    grad_part, sums1 = pl.pallas_call(
        last_kernel,
        grid_spec=pltpu.PrefetchScalarGridSpec(
            num_scalar_prefetch=1,
            grid=(blocks,),
            in_specs=[
                segment_spec(back), rows_spec(width, back), stack_spec(3, half, back), stack_spec(3, half, back),
                whole((width, half)), whole((width, half)), whole((width, half)), whole((3, width, half)),
                bound_spec(back), whole((8, width)),
            ],
            out_specs=[rows_spec(width, back), whole((8, width))],
            scratch_shapes=[pltpu.VMEM((1, width), F32)],
        ),
        out_shape=[shape((length, width), BF16), shape((8, width), F32)],
        compiler_params=params(48),
        name="time_mix_back",
    )(
        meta, tokens, d_middle, d_own, d_far, key_weight, value_weight, receptance_weight, far_kvr,
        bounds1, vectors1,
    )

    def both(own, far):
        return jnp.where(side == 0, jnp.stack([own, far]), jnp.stack([far, own]))

    grad_tokens = both(grad_part, swapped(grad_part)).astype(F32)
    mixed_own, mixed_far = halves(mixed, 1)
    mixed_out = both(mixed_own, swapped(mixed_far))

    back_states = swapped(final_far)
    finals = [both(final_own[n], back_states[n]) for n in range(3)]
    last_rows = jnp.concatenate([last_att, last_ffn])
    last_rows = both(last_rows, swapped(last_rows))

    def full(own, far):
        return jnp.where(side == 0, jnp.concatenate([own, far]), jnp.concatenate([far, own]))

    small = jnp.concatenate([
        sums1[0:2], sums2[0:2], sums1[2:5], sums2[2:4],
        jnp.stack([full(channel_sums_own[n], channel_sums_far[n]) for n in range(2)]),
    ])
    small = summed_everywhere(small, size)

    big = [scattered_sum(own, far, size, groups) for own, far in (g_ck, g_cv, g_cr, g_wo, g_kvr)]
    return (
        (mixed_out, grad_tokens, *finals, last_rows[:, 0], last_rows[:, 1])
        + tuple(small[n] for n in range(11))
        + tuple(big[4][:, n * half : (n + 1) * half] for n in range(3))
        + (big[3].T, big[0], big[2], big[1].T)
    )


def solution(mesh):
    split = P("dp", "tensor")
    turned = P("tensor", "dp")
    return jax.shard_map(
        functools.partial(shards, mesh.shape["dp"]),
        mesh=mesh,
        in_specs=(P("dp"), P("dp"), P("dp"), P("dp"), split, split, split)
        + (P(),) * 9
        + (P("tensor"), P("tensor"))
        + (P(None, "tensor"),) * 3
        + (P("tensor"), P(None, "tensor"), P(None, "tensor"), P("tensor")),
        out_specs=(P("dp", None, "tensor"), P("dp"), split, split, split, P("dp"), P("dp"))
        + (P(),) * 11
        + (split, split, split, turned, split, split, turned),
        check_vma=False,
    )
```

time: 1860 us -> 437 us (0.23)
  waiting for transfers between devices: 825 us -> 184 us
  other arithmetic: 624 us -> 27.7 us
  local copies, waits for them, and re-layouts: 185 us -> 36 us
  matrix products: 133 us -> 0 us
  Pallas kernels: 0 us -> 126 us
  starting transfers between devices: 10.3 us -> 53.5 us
  blocking collectives: 41.5 us -> 0 us
    reduce_scatter x7 -> x0, waiting for transfers between devices: 449 us -> none  [the longest x1 79.6 us: shards(): lax.psum_scatter(channel_key_gradient, 'dp', scatter_dimension=0, tiled=T...]
    reduce_sum x424 -> x0, other arithmetic: 330 us -> none  [the longest x64 102 us: advance(): jnp.sum(weights * value_block[:, None, :, :], axis=2)]
    psum x3 -> x0, waiting for transfers between devices: 309 us -> none  [the longest x1 155 us: shards(): lax.psum(contract_product('znb,bk->znk', gated_reduced, output_weight), '...]
    ppermute x0 -> x54, waiting for transfers between devices: none -> 184 us  [the longest x18 152 us: swapped(): return lax.ppermute(array, 'tensor', [(0, 1), (1, 0)])]
    dot_general x21 -> x0, matrix products: 133 us -> none  [contract_product(): return jnp.einsum(form, left, right, preferred_element_type=jnp.float32)]
    pallas_call x0 -> x17, Pallas kernels: none -> 126 us  [the longest x1 36 us: shards(): pl.pallas_call(channel_kernel, grid_spec=pltpu.PrefetchScalarGridSpec(num...]
    squeeze x128 -> x0, local copies, waits for them, and re-layouts: 104 us -> none  [weighted_value_blocks(): lax.scan(advance, (numerator_begin, denominator_begin, maximum_begin), (b...]
    dynamic_update_slice x97 -> x0, other arithmetic: 101 us -> none  [the longest x96 101 us: weighted_value_blocks(): lax.scan(advance, (numerator_begin, denominator_begin, maximum_begin), (b...]
  transfers between devices with their start and end apart: 12 -> 54, of which waited for: 11 -> 21; matrix products, arithmetic and copies ran while one was open for 4% -> 10% of each run, Pallas kernels for 0% -> 12%
where the time goes in v1:
time: 437 us; the launch traced here: 429 us
  waiting for transfers between devices  184 us (42%)
  Pallas kernels  126 us (29%)
  starting transfers between devices  53.5 us (12%)
  local copies, waits for them, and re-layouts  36 us (8%)
  other arithmetic  27.7 us (6%)
    ppermute x18, waiting for transfers between devices, swapped(): return lax.ppermute(array, 'tensor', [(0, 1), (1, 0)])  152 us
    pallas_call x1, Pallas kernels, shards(): pl.pallas_call(channel_kernel, grid_spec=pltpu.PrefetchScalarGridSpec(num...  36 us
    pallas_call x10, Pallas kernels, weight_gradient(): pl.pallas_call(functools.partial(weight_gradient_kernel, order, groups),...  35.6 us
    ppermute x36, starting transfers between devices, crossed(): return lax.ppermute(array, 'dp', [(n, n ^ bit) for n in range(size)])  33.2 us
    ppermute x36, waiting for transfers between devices, crossed(): return lax.ppermute(array, 'dp', [(n, n ^ bit) for n in range(size)])  31.9 us
    ppermute x18, starting transfers between devices, swapped(): return lax.ppermute(array, 'tensor', [(0, 1), (1, 0)])  20.2 us
    unnamed x140, local copies, waits for them, and re-layouts  16.3 us
    pallas_call x1, Pallas kernels, shards(): pl.pallas_call(last_kernel, grid_spec=pltpu.PrefetchScalarGridSpec(num_sc...  13.5 us
  transfers between devices with their start and end apart: 54, of which 21 were waited for; matrix products, arithmetic and copies ran while one was open for 10% of the time, Pallas kernels for 12%

profile of v1, /device:TPU:0, one launch (start us, length us, event | category | flops | bytes accessed | tf_op | source)
XLA Modules:
  0.0 429.3 jit_solution(14925118893219069973)
XLA Ops:
  14.6 11.9 %time_mix_own.1 = (bf16[3,1024,768]{2,1,0:T(8,128)(2,1)}, f32[4,8,768]{2,1,0:T(8,128)S(1)}, f32[1,768]{1,0:T(1,128)S(1)}, bf16[1024,384]{1,0:T(8,128)(2,1)S(1)},...) custom-call(s32[2]{0:T(128)S(1)} %pad_add_fusion.meta, ...), custom_call_target="tpu_custom_call" | custom-call | tf_op jit(solution)/shard_map/time_mix_own/pallas_call | solution.py:558
  36.4 27.7 %collective-permute-done.13 = bf16[384,384]{1,0:T(8,128)(2,1)} collective-permute-done((bf16[384,384]{1,0:T(8,128)(2,1)S(1)}, bf16[384,384]{1,0:T(8,128)(2,1)}, u32[]{:S(2)}, u32[]{:S(2)}) %collective-permute-start.13) | collective-permute-done | bytes 294944 | tf_op jit(solution)/shard_map/ppermute | solution.py:430
  67.7 21.1 %collective-permute-done.6.channel_ref = f32[8,384]{1,0:T(8,128)S(1)} collective-permute-done((f32[8,384]{1,0:T(8,128)S(1)}, f32[8,384]{1,0:T(8,128)S(1)}, u32[]{:S(2)}, u32[]{:S(2)}) %collective-permute-start.6) | collective-permute-done | bytes 12320 | tf_op jit(solution)/shard_map/ppermute | solution.py:430
  88.7 9.6 %time_mix_far.1 = (bf16[1024,384]{1,0:T(8,128)(2,1)S(1)}, f32[7,1024,384]{2,1,0:T(8,128)}, f32[2,128,384]{2,1,0:T(8,128)S(1)}, f32[8,384]{1,0:T(8,128)S(1)}) custom-call(bf16[3,1024,768]{2,1,0:T(8,128)(2,1)} %get-tuple-element.59.mix_ref.left_ref, bf16[3,768,384]{2,1,0:T(8,128)(2,1)S(1)} %pad_maximum_fusion.weight_ref, ...), custom_call_target="tpu_custom_call" | custom-call | tf_op jit(solution)/shard_map/time_mix_far/pallas_call | solution.py:574
  100.1 7.0 %middle.1 = (f32[1024,768]{1,0:T(8,128)S(1)}, bf16[2,1024,768]{2,1,0:T(8,128)(2,1)}, f32[4,8,768]{2,1,0:T(8,128)S(1)}, f32[1,768]{1,0:T(1,128)S(1)}) custom-call(s32[2]{0:T(128)S(1)} %pad_add_fusion.meta, bf16[2,1024,768]{2,1,0:T(8,128)(2,1)} %tokens_ref.5, bf16[1024,384]{1,0:T(8,128)(2,1)S(1)} %copy-done.20, ...), custom_call_target="tpu_custom_call" | custom-call | tf_op jit(solution)/shard_map/middle/pallas_call | solution.py:585
  107.1 4.4 %fusion.2 = (bf16[1,1024,768]{2,1,0:T(8,128)(2,1)S(1)}, bf16[1,1024,768]{2,1,0:T(8,128)(2,1)}) fusion(bf16[2,1024,768]{2,1,0:T(8,128)(2,1)} %get-tuple-element.62.mix_ref), kind=kLoop, calls=%fused_computation.83 | loop fusion | bytes 6291456 | tf_op jit(solution)/shard_map/slice | solution.py:647
  124.1 36.0 %channel_mix.1 = (bf16[1024,768]{1,0:T(8,128)(2,1)}, bf16[1024,1536]{1,0:T(8,128)(2,1)}, bf16[1024,1536]{1,0:T(8,128)(2,1)}, bf16[1024,1536]{1,0:T(8,128)(2,1)},...) custom-call(s32[2]{0:T(128)} %copy-done.39, ...), custom_call_target="tpu_custom_call" | custom-call | tf_op jit(solution)/shard_map/channel_mix/pallas_call | solution.py:605
  161.6 6.1 %scan_back.2 = (bf16[3,1024,384]{2,1,0:T(8,128)(2,1)S(1)}, f32[8,384]{1,0:T(8,128)S(1)}) custom-call(f32[1024,384]{1,0:T(8,128)S(1)} %copy-done.32, f32[7,1024,384]{2,1,0:T(8,128)} %get-tuple-element.67.save_ref, f32[2,128,384]{2,1,0:T(8,128)S(1)} %copy-done.34, f32[8,384]{1,0:T(8,128)S(1)} %stack.143.channel_ref), custom_call_target="tpu_custom_call" | custom-call | tf_op jit(solution)/shard_map/scan_back/pallas_call | solution.py:651
  171.0 5.0 %weight_gradient.10 = bf16[768,1152]{1,0:T(8,128)(2,1)S(1)} custom-call(s32[2]{0:T(128)S(1)} %copy-done.40, bf16[3,1024,768]{2,1,0:T(8,128)(2,1)S(1)} %copy-done.2, bf16[3,1024,384]{2,1,0:T(8,128)(2,1)S(1)} %get-tuple-element.69.own_ref.right_ref), custom_call_target="tpu_custom_call" | custom-call | flops 1811939328 | bytes 9437184 | tf_op jit(solution)/shard_map/weight_gradient/pallas_call | solution.py:408
  177.2 6.2 %scan_back.3 = (bf16[3,1024,384]{2,1,0:T(8,128)(2,1)S(1)}, f32[8,384]{1,0:T(8,128)S(1)}) custom-call(f32[1024,384]{1,0:T(8,128)S(1)} %copy-done.31, f32[7,1024,384]{2,1,0:T(8,128)} %get-tuple-element.71.save_ref, f32[2,128,384]{2,1,0:T(8,128)S(1)} %copy-done.36, f32[8,384]{1,0:T(8,128)S(1)} %collective-permute-done.6.channel_ref), custom_call_target="tpu_custom_call" | custom-call | tf_op jit(solution)/shard_map/scan_back/pallas_call | solution.py:651
  183.5 4.9 %weight_gradient.11 = bf16[768,1152]{1,0:T(8,128)(2,1)S(1)} custom-call(s32[2]{0:T(128)S(1)} %copy-done.40, bf16[3,1024,768]{2,1,0:T(8,128)(2,1)S(1)} %bitcast.39, bf16[3,1024,384]{2,1,0:T(8,128)(2,1)S(1)} %get-tuple-element.73.far_ref.right_ref), custom_call_target="tpu_custom_call" | custom-call | flops 1811939328 | bytes 9437184 | tf_op jit(solution)/shard_map/weight_gradient/pallas_call | solution.py:408
  189.7 13.5 %time_mix_back.1 = (bf16[1024,768]{1,0:T(8,128)(2,1)S(1)}, f32[8,768]{1,0:T(8,128)S(1)}) custom-call(s32[2]{0:T(128)S(1)} %copy-done.40, bf16[2,1024,768]{2,1,0:T(8,128)(2,1)} %tokens_ref.5, f32[1024,768]{1,0:T(8,128)} %get-tuple-element.65.dmid_ref, bf16[3,1024,384]{2,1,0:T(8,128)(2,1)} %copy-done.3, bf16[3,1024,384]{2,1,0:T(8,128)(2,1)} %copy-done.4, ...), custom_call_target="tpu_custom_call" | custom-call | tf_op jit(solution)/shard_map/time_mix_back/pallas_call | solution.py:670
  203.3 4.4 %weight_gradient.18 = bf16[768,1536]{1,0:T(8,128)(2,1)S(1)} custom-call(s32[2]{0:T(128)S(1)} %copy-done.40, bf16[1,1024,768]{2,1,0:T(8,128)(2,1)S(1)} %bitcast.49, bf16[1,1024,1536]{2,1,0:T(8,128)(2,1)S(1)} %bitcast.48), custom_call_target="tpu_custom_call" | custom-call | flops 2415919104 | bytes 3145728 | tf_op jit(solution)/shard_map/weight_gradient/pallas_call | solution.py:408
  209.6 4.4 %weight_gradient.19 = bf16[768,1536]{1,0:T(8,128)(2,1)S(1)} custom-call(s32[2]{0:T(128)S(1)} %copy-done.40, bf16[1,1024,768]{2,1,0:T(8,128)(2,1)S(1)} %bitcast.50, bf16[1,1024,1536]{2,1,0:T(8,128)(2,1)S(1)} %bitcast.47), custom_call_target="tpu_custom_call" | custom-call | flops 2415919104 | bytes 3145728 | tf_op jit(solution)/shard_map/weight_gradient/pallas_call | solution.py:408
  226.8 4.4 %weight_gradient.14 = bf16[768,1536]{1,0:T(8,128)(2,1)S(1)} custom-call(s32[2]{0:T(128)S(1)} %copy-done.40, bf16[1,1024,768]{2,1,0:T(8,128)(2,1)S(1)} %copy-done.30, bf16[1,1024,1536]{2,1,0:T(8,128)(2,1)S(1)} %bitcast.46), custom_call_target="tpu_custom_call" | custom-call | flops 2415919104 | bytes 3145728 | tf_op jit(solution)/shard_map/weight_gradient/pallas_call | solution.py:408
  233.1 4.7 %weight_gradient.15 = bf16[768,1536]{1,0:T(8,128)(2,1)S(1)} custom-call(s32[2]{0:T(128)S(1)} %copy-done.40, bf16[1,1024,768]{2,1,0:T(8,128)(2,1)S(1)} %copy-done.30, bf16[1,1024,1536]{2,1,0:T(8,128)(2,1)S(1)} %bitcast.45), custom_call_target="tpu_custom_call" | custom-call | flops 2415919104 | bytes 3145728 | tf_op jit(solution)/shard_map/weight_gradient/pallas_call | solution.py:408
  255.6 6.9 %collective-permute-done.44 = bf16[384,384]{1,0:T(8,128)(2,1)S(1)} collective-permute-done((bf16[384,384]{1,0:T(8,128)(2,1)S(1)}, bf16[384,384]{1,0:T(8,128)(2,1)S(1)}, u32[]{:S(2)}, u32[]{:S(2)}) %collective-permute-start.44) | collective-permute-done | bytes 294944 | tf_op jit(solution)/shard_map/ppermute | solution.py:430
  264.1 4.7 %collective-permute-done.32 = bf16[384,384]{1,0:T(8,128)(2,1)S(1)} collective-permute-done((bf16[384,384]{1,0:T(8,128)(2,1)S(1)}, bf16[384,384]{1,0:T(8,128)(2,1)S(1)}, u32[]{:S(2)}, u32[]{:S(2)}) %collective-permute-start.32) | collective-permute-done | bytes 294944 | tf_op jit(solution)/shard_map/ppermute | solution.py:430
  279.2 6.1 %collective-permute-done.15 = bf16[1024,384]{1,0:T(8,128)(2,1)S(1)} collective-permute-done((bf16[1024,384]{1,0:T(8,128)(2,1)S(1)}, bf16[1024,384]{1,0:T(8,128)(2,1)S(1)}, u32[]{:S(2)}, u32[]{:S(2)}) %collective-permute-start.15) | collective-permute-done | bytes 786464 | tf_op jit(solution)/shard_map/ppermute | solution.py:430
  302.7 18.7 %collective-permute-done.26 = bf16[384,1152]{1,0:T(8,128)(2,1)S(1)} collective-permute-done((bf16[384,1152]{1,0:T(8,128)(2,1)S(1)}, bf16[384,1152]{1,0:T(8,128)(2,1)S(1)}, u32[]{:S(2)}, u32[]{:S(2)}) %collective-permute-start.26) | collective-permute-done | bytes 884768 | tf_op jit(solution)/shard_map/ppermute | solution.py:430
  324.1 31.0 %collective-permute-done.16 = bf16[1024,768]{1,0:T(8,128)(2,1)S(1)} collective-permute-done((bf16[1024,768]{1,0:T(8,128)(2,1)S(1)}, bf16[1024,768]{1,0:T(8,128)(2,1)S(1)}, u32[]{:S(2)}, u32[]{:S(2)}) %collective-permute-start.16) | collective-permute-done | bytes 1572896 | tf_op jit(solution)/shard_map/ppermute | solution.py:430
  360.4 20.0 %collective-permute-done.50 = bf16[384,1536]{1,0:T(8,128)(2,1)S(1)} collective-permute-done((bf16[384,1536]{1,0:T(8,128)(2,1)S(1)}, bf16[384,1536]{1,0:T(8,128)(2,1)S(1)}, u32[]{:S(2)}, u32[]{:S(2)}) %collective-permute-start.50) | collective-permute-done | bytes 1179680 | tf_op jit(solution)/shard_map/ppermute | solution.py:430
  385.3 15.6 %collective-permute-done.38 = bf16[384,1536]{1,0:T(8,128)(2,1)S(1)} collective-permute-done((bf16[384,1536]{1,0:T(8,128)(2,1)S(1)}, bf16[384,1536]{1,0:T(8,128)(2,1)S(1)}, u32[]{:S(2)}, u32[]{:S(2)}) %collective-permute-start.38) | collective-permute-done | bytes 1179680 | tf_op jit(solution)/shard_map/ppermute | solution.py:430
  405.5 6.5 %collective-permute-done.39 = bf16[192,1536]{1,0:T(8,128)(2,1)S(1)} collective-permute-done((bf16[192,1536]{1,0:T(8,128)(2,1)S(1)}, bf16[192,1536]{1,0:T(8,128)(2,1)S(1)}, u32[]{:S(2)}, u32[]{:S(2)}) %collective-permute-start.39) | collective-permute-done | bytes 589856 | tf_op jit(solution)/shard_map/ppermute | solution.py:434
  (360 shorter events, 145.9 us)
Async XLA Ops:
  2.5 25.7 %collective-permute-start = (bf16[384,384]{1,0:T(8,128)(2,1)}, bf16[384,384]{1,0:T(8,128)(2,1)}, u32[]{:S(2)}, u32[]{:S(2)}) collective-permute-start(bf16[384,384]{1,0:T(8,128)(2,1)} %constant_dynamic-slice_fusion.11), channel_id=1, source_target_pairs={{0,1},{1,0},{2,3},{3,2},{4,5},{5,4},{6,7},{7,6},{8,9},{9,8},{10,11... | collective-permute-start | bytes 884744 | tf_op jit(solution)/shard_map/ppermute | solution.py:430
  6.4 24.3 %collective-permute-start.2 = (bf16[384,384]{1,0:T(8,128)(2,1)S(1)}, bf16[384,384]{1,0:T(8,128)(2,1)}, u32[]{:S(2)}, u32[]{:S(2)}) collective-permute-start(bf16[384,384]{1,0:T(8,128)(2,1)S(1)} %constant_dynamic-slice_fusion.10), channel_id=1, source_target_pairs={{0,1},{1,0},{2,3},{3,2},{4,5},{5,4},{6,7},{7,6},{8,9},{9,8},{10,11... | collective-permute-start | bytes 884744 | tf_op jit(solution)/shard_map/ppermute | solution.py:430
  7.7 23.5 %collective-permute-start.4 = (bf16[384,384]{1,0:T(8,128)(2,1)S(1)}, bf16[384,384]{1,0:T(8,128)(2,1)}, u32[]{:S(2)}, u32[]{:S(2)}) collective-permute-start(bf16[384,384]{1,0:T(8,128)(2,1)S(1)} %constant_dynamic-slice_fusion.9), channel_id=1, source_target_pairs={{0,1},{1,0},{2,3},{3,2},{4,5},{5,4},{6,7},{7,6},{8,9},{9,8},{10,11... | collective-permute-start | bytes 884744 | tf_op jit(solution)/shard_map/ppermute | solution.py:430
  9.8 23.2 %collective-permute-start.7 = (bf16[192,768]{1,0:T(8,128)(2,1)S(1)}, bf16[192,768]{1,0:T(8,128)(2,1)}, u32[]{:S(2)}, u32[]{:S(2)}) collective-permute-start(bf16[192,768]{1,0:T(8,128)(2,1)S(1)} %constant_dynamic-slice_fusion.5), channel_id=1, source_target_pairs={{0,1},{1,0},{2,3},{3,2},{4,5},{5,4},{6,7},{7,6},{8,9},{9,8},{10,11... | collective-permute-start | bytes 884744 | tf_op jit(solution)/shard_map/ppermute | solution.py:430
  12.2 99.3 %collective-permute-start.9 = (bf16[384,1536]{1,0:T(8,128)(2,1)}, bf16[384,1536]{1,0:T(8,128)(2,1)}, u32[]{:S(2)}, u32[]{:S(2)}) collective-permute-start(bf16[384,1536]{1,0:T(8,128)(2,1)} %constant_dynamic-slice_fusion.3), channel_id=1, source_target_pairs={{0,1},{1,0},{2,3},{3,2},{4,5},{5,4},{6,7},{7,6},{8,9},{9,8},{10,11... | collective-permute-start | bytes 3538952 | tf_op jit(solution)/shard_map/ppermute | solution.py:430
  31.2 32.9 %collective-permute-start.13 = (bf16[384,384]{1,0:T(8,128)(2,1)S(1)}, bf16[384,384]{1,0:T(8,128)(2,1)}, u32[]{:S(2)}, u32[]{:S(2)}) collective-permute-start(bf16[384,384]{1,0:T(8,128)(2,1)S(1)} %constant_dynamic-slice_fusion.1), channel_id=1, source_target_pairs={{0,1},{1,0},{2,3},{3,2},{4,5},{5,4},{6,7},{7,6},{8,9},{9,8},{10,11... | collective-permute-start | bytes 884744 | tf_op jit(solution)/shard_map/ppermute | solution.py:430
  31.3 34.9 %collective-permute-start.5 = (bf16[384,384]{1,0:T(8,128)(2,1)}, bf16[384,384]{1,0:T(8,128)(2,1)S(1)}, u32[]{:S(2)}, u32[]{:S(2)}) collective-permute-start(bf16[384,384]{1,0:T(8,128)(2,1)} %collective-permute-done.4), channel_id=1, source_target_pairs={{0,2},{2,0},{4,6},{6,4},{8,10},{10,8},{12,14},{14,12},{16,18},{18,... | collective-permute-start | bytes 884744 | tf_op jit(solution)/shard_map/ppermute | solution.py:434
  32.9 83.4 %collective-permute-start.11 = (bf16[768,768]{1,0:T(8,128)(2,1)}, bf16[768,768]{1,0:T(8,128)(2,1)S(1)}, u32[]{:S(2)}, u32[]{:S(2)}) collective-permute-start(bf16[768,768]{1,0:T(8,128)(2,1)} %constant_dynamic-slice_fusion.2), channel_id=1, source_target_pairs={{0,1},{1,0},{2,3},{3,2},{4,5},{5,4},{6,7},{7,6},{8,9},{9,8},{10,11... | collective-permute-start | bytes 3538952 | tf_op jit(solution)/shard_map/ppermute | solution.py:430
  34.8 63.5 %collective-permute-start.8 = (bf16[192,768]{1,0:T(8,128)(2,1)}, bf16[192,768]{1,0:T(8,128)(2,1)S(1)}, u32[]{:S(2)}, u32[]{:S(2)}) collective-permute-start(bf16[192,768]{1,0:T(8,128)(2,1)} %collective-permute-done.7), channel_id=1, source_target_pairs={{0,2},{2,0},{4,6},{6,4},{8,10},{10,8},{12,14},{14,12},{16,18},{18,... | collective-permute-start | bytes 884744 | tf_op jit(solution)/shard_map/ppermute | solution.py:434
  64.1 24.6 %collective-permute-start.6 = (f32[8,384]{1,0:T(8,128)S(1)}, f32[8,384]{1,0:T(8,128)S(1)}, u32[]{:S(2)}, u32[]{:S(2)}) collective-permute-start(f32[8,384]{1,0:T(8,128)S(1)} %stack.145), channel_id=1, source_target_pairs={{0,1},{1,0},{2,3},{3,2},{4,5},{5,4},{6,7},{7,6},{8,9},{9,8},{10,11... | collective-permute-start | bytes 36872 | tf_op jit(solution)/shard_map/ppermute | solution.py:430
  66.2 47.5 %collective-permute-start.14 = (bf16[384,384]{1,0:T(8,128)(2,1)}, bf16[384,384]{1,0:T(8,128)(2,1)S(1)}, u32[]{:S(2)}, u32[]{:S(2)}) collective-permute-start(bf16[384,384]{1,0:T(8,128)(2,1)} %collective-permute-done.13), channel_id=1, source_target_pairs={{0,2},{2,0},{4,6},{6,4},{8,10},{10,8},{12,14},{14,12},{16,18},{18,... | collective-permute-start | bytes 884744 | tf_op jit(solution)/shard_map/ppermute | solution.py:434
  209.0 151.4 %collective-permute-start.48 = (bf16[384,1536]{1,0:T(8,128)(2,1)}, bf16[384,1536]{1,0:T(8,128)(2,1)}, u32[]{:S(2)}, u32[]{:S(2)}) collective-permute-start(bf16[384,1536]{1,0:T(8,128)(2,1)} %slice.390), channel_id=1, source_target_pairs={{0,2},{2,0},{4,6},{6,4},{8,10},{10,8},{12,14},{14,12},{16,18},{18,... | collective-permute-start | bytes 3538952 | tf_op jit(solution)/shard_map/ppermute | solution.py:434
  219.4 33.1 %collective-permute-start.43 = (bf16[384,384]{1,0:T(8,128)(2,1)}, bf16[384,384]{1,0:T(8,128)(2,1)S(1)}, u32[]{:S(2)}, u32[]{:S(2)}) collective-permute-start(bf16[384,384]{1,0:T(8,128)(2,1)} %slice.382), channel_id=1, source_target_pairs={{0,2},{2,0},{4,6},{6,4},{8,10},{10,8},{12,14},{14,12},{16,18},{18,... | collective-permute-start | bytes 884744 | tf_op jit(solution)/shard_map/ppermute | solution.py:434
  222.7 32.9 %collective-permute-start.42 = (bf16[384,384]{1,0:T(8,128)(2,1)}, bf16[384,384]{1,0:T(8,128)(2,1)}, u32[]{:S(2)}, u32[]{:S(2)}) collective-permute-start(bf16[384,384]{1,0:T(8,128)(2,1)} %slice.380), channel_id=1, source_target_pairs={{0,2},{2,0},{4,6},{6,4},{8,10},{10,8},{12,14},{14,12},{16,18},{18,... | collective-permute-start | bytes 884744 | tf_op jit(solution)/shard_map/ppermute | solution.py:434
  255.6 45.5 %collective-permute-start.49 = (bf16[384,1536]{1,0:T(8,128)(2,1)S(1)}, bf16[384,1536]{1,0:T(8,128)(2,1)S(1)}, u32[]{:S(2)}, u32[]{:S(2)}) collective-permute-start(bf16[384,1536]{1,0:T(8,128)(2,1)S(1)} %copy-done.50), channel_id=1, source_target_pairs={{0,2},{2,0},{4,6},{6,4},{8,10},{10,8},{12,14},{14,12},{16,18},{18,... | collective-permute-start | bytes 3538952 | tf_op jit(solution)/shard_map/ppermute | solution.py:434
  262.5 22.8 %collective-permute-start.15 = (bf16[1024,384]{1,0:T(8,128)(2,1)S(1)}, bf16[1024,384]{1,0:T(8,128)(2,1)S(1)}, u32[]{:S(2)}, u32[]{:S(2)}) collective-permute-start(bf16[1024,384]{1,0:T(8,128)(2,1)S(1)} %get-tuple-element.107), channel_id=1, source_target_pairs={{0,1},{1,0},{2,3},{3,2},{4,5},{5,4},{6,7},{7,6},{8,9},{9,8},{10,11... | collective-permute-start | bytes 2359304 | tf_op jit(solution)/shard_map/ppermute | solution.py:430
  264.1 31.4 %collective-permute-start.25 = (bf16[384,1152]{1,0:T(8,128)(2,1)S(1)}, bf16[384,1152]{1,0:T(8,128)(2,1)S(1)}, u32[]{:S(2)}, u32[]{:S(2)}) collective-permute-start(bf16[384,1152]{1,0:T(8,128)(2,1)S(1)} %slice.349), channel_id=1, source_target_pairs={{0,2},{2,0},{4,6},{6,4},{8,10},{10,8},{12,14},{14,12},{16,18},{18,... | collective-permute-start | bytes 2654216 | tf_op jit(solution)/shard_map/ppermute | solution.py:434
  279.1 23.3 %collective-permute-start.24 = (bf16[384,1152]{1,0:T(8,128)(2,1)S(1)}, bf16[384,1152]{1,0:T(8,128)(2,1)S(1)}, u32[]{:S(2)}, u32[]{:S(2)}) collective-permute-start(bf16[384,1152]{1,0:T(8,128)(2,1)S(1)} %slice.347), channel_id=1, source_target_pairs={{0,2},{2,0},{4,6},{6,4},{8,10},{10,8},{12,14},{14,12},{16,18},{18,... | collective-permute-start | bytes 2654216 | tf_op jit(solution)/shard_map/ppermute | solution.py:434
  301.0 54.1 %collective-permute-start.16 = (bf16[1024,768]{1,0:T(8,128)(2,1)S(1)}, bf16[1024,768]{1,0:T(8,128)(2,1)S(1)}, u32[]{:S(2)}, u32[]{:S(2)}) collective-permute-start(bf16[1024,768]{1,0:T(8,128)(2,1)S(1)} %copy-done.29), channel_id=1, source_target_pairs={{0,1},{1,0},{2,3},{3,2},{4,5},{5,4},{6,7},{7,6},{8,9},{9,8},{10,11... | collective-permute-start | bytes 4718600 | tf_op jit(solution)/shard_map/ppermute | solution.py:430
  302.4 82.9 %collective-permute-start.36 = (bf16[384,1536]{1,0:T(8,128)(2,1)S(1)}, bf16[384,1536]{1,0:T(8,128)(2,1)S(1)}, u32[]{:S(2)}, u32[]{:S(2)}) collective-permute-start(bf16[384,1536]{1,0:T(8,128)(2,1)S(1)} %slice.370), channel_id=1, source_target_pairs={{0,2},{2,0},{4,6},{6,4},{8,10},{10,8},{12,14},{14,12},{16,18},{18,... | collective-permute-start | bytes 3538952 | tf_op jit(solution)/shard_map/ppermute | solution.py:434
  321.4 59.0 %collective-permute-start.50 = (bf16[384,1536]{1,0:T(8,128)(2,1)S(1)}, bf16[384,1536]{1,0:T(8,128)(2,1)S(1)}, u32[]{:S(2)}, u32[]{:S(2)}) collective-permute-start(bf16[384,1536]{1,0:T(8,128)(2,1)S(1)} %add_convert_fusion.1), channel_id=1, source_target_pairs={{0,1},{1,0},{2,3},{3,2},{4,5},{5,4},{6,7},{7,6},{8,9},{9,8},{10,11... | collective-permute-start | bytes 3538952 | tf_op jit(solution)/shard_map/ppermute | solution.py:430
  322.2 36.4 %collective-permute-start.27 = (bf16[192,1152]{1,0:T(8,128)(2,1)S(1)}, bf16[192,1152]{1,0:T(8,128)(2,1)S(1)}, u32[]{:S(2)}, u32[]{:S(2)}) collective-permute-start(bf16[192,1152]{1,0:T(8,128)(2,1)S(1)} %slice.351), channel_id=1, source_target_pairs={{0,4},{2,6},{4,0},{6,2},{8,12},{10,14},{12,8},{14,10},{16,20},{18,... | collective-permute-start | bytes 1327112 | tf_op jit(solution)/shard_map/ppermute | solution.py:434
  355.1 45.8 %collective-permute-start.38 = (bf16[384,1536]{1,0:T(8,128)(2,1)S(1)}, bf16[384,1536]{1,0:T(8,128)(2,1)S(1)}, u32[]{:S(2)}, u32[]{:S(2)}) collective-permute-start(bf16[384,1536]{1,0:T(8,128)(2,1)S(1)} %add_convert_fusion.4), channel_id=1, source_target_pairs={{0,1},{1,0},{2,3},{3,2},{4,5},{5,4},{6,7},{7,6},{8,9},{9,8},{10,11... | collective-permute-start | bytes 3538952 | tf_op jit(solution)/shard_map/ppermute | solution.py:430
  358.7 25.0 %collective-permute-start.28 = (bf16[96,1152]{1,0:T(8,128)(2,1)S(1)}, bf16[96,1152]{1,0:T(8,128)(2,1)S(1)}, u32[]{:S(2)}, u32[]{:S(2)}) collective-permute-start(bf16[96,1152]{1,0:T(8,128)(2,1)S(1)} %slice.353), channel_id=1, source_target_pairs={{0,8},{2,10},{4,12},{6,14},{8,0},{10,2},{12,4},{14,6},{16,24},{18,... | collective-permute-start | bytes 663560 | tf_op jit(solution)/shard_map/ppermute | solution.py:434
  (99 other events, 842.8 us)
